TPU v7x, 32 devices: a whole 2x2x4 slice. The times are simulated.
32 devices in a mesh: req: 4 (over z), exp: 8 (over y, x, core).
Axes of the slice: x: 2, y: 2, z: 4, core: 2. Of those that a mesh axis runs over, the one named last changes fastest.
Arguments:
- hidden_in: bfloat16 [4096, 1024], P(('req', 'exp')), may hold values from -3 to 3
- queries: bfloat16 [4096, 1024], P(('req', 'exp')), may hold values from -9.5 to 9.5
- suffix_kv: bfloat16 [4096, 2048], P(('req', 'exp')), may hold values from -9.5 to 9.5
- request_ids: int32 [4096], P(('req', 'exp')), may hold values from 0 to 63, never falling along the last dimension, each value on 1 to 128 neighbouring positions
- group_of_request: int32 [64], replicated, may hold values from 0 to 3
- page_pool: bfloat16 [32, 128, 2048], P('exp'), may hold values from -9.5 to 9.5
- page_table: int32 [4, 8], replicated, may hold values from 0 to 31, as said below
- out_proj: bfloat16 [1024, 1024], replicated, may hold values from -0.1875 to 0.1875
- norm_gain: float32 [1024], replicated, may hold values from 0.1 to 1.9
- routes: int32 [4096, 2], P(('req', 'exp')), may hold values from 0 to 7, all different within a row; in each aligned block of 128 rows (0 to 127, 128 to 255, ...) at most 40 rows name the same one
- route_gates: float32 [4096, 2], P(('req', 'exp')), may hold values from 0.2 to 1
- w_gate: bfloat16 [8, 1024, 2816], P('exp'), may hold values from -0.1875 to 0.1875
- w_up: bfloat16 [8, 1024, 2816], P('exp'), may hold values from -0.1875 to 0.1875
- w_down: bfloat16 [8, 2816, 1024], P('exp'), may hold values from -0.109375 to 0.109375
Outputs:
- mixed: bfloat16 [4096, 1024], P(('req', 'exp'))
- layer_out: bfloat16 [4096, 1024], P(('req', 'exp'))
Inputs may be any that keep to these rules, and one draw needn't show every extreme that they name: `request_ids`: ids never fall; each request has 1 to 128 consecutive tokens, one exactly 128. `page_table`: every page of the pool appears exactly once in the table. `routes`: each token names 2 different experts; in each aligned block of 128 tokens no expert is named more than 40 times, a bound that some block reaches.
All inputs are finite; a program needn't handle non-finite values.
Results may differ from a plain program's by a relative error of at most 0.015.
Values may be sent and summed in bfloat16 or wider, within the bound.
A program may use at most 192 MiB of HBM per device.

v0:
```python
import math

import jax
import jax.numpy as jnp
from jax import lax
from jax.sharding import PartitionSpec as P

H = 16
HD = 64
PAGE = 128
POOL_DEV = 4


MASKED = -1e30


def from_behind(value, axis, by):
    count = lax.axis_size(axis)
    pairs = [(i, i + by) for i in range(count) if 0 <= i + by < count]
    return lax.ppermute(value, axis, pairs)


def partial_attend(query_heads, key_heads, value_heads, allowed):
    scaled = jnp.einsum(
        "qhd,khd->qhk", query_heads, key_heads, preferred_element_type=jnp.float32
    ) * (1.0 / math.sqrt(HD))
    allowed_heads = allowed[:, None, :]
    scaled = jnp.where(allowed_heads, scaled, MASKED)
    highest = jnp.max(scaled, axis=-1)
    weights = jnp.where(allowed_heads, jnp.exp(scaled - highest[..., None]), 0.0)
    totals = jnp.sum(weights, axis=-1)
    summed = jnp.einsum(
        "qhk,khd->qhd",
        weights.astype(jnp.bfloat16),
        value_heads,
        preferred_element_type=jnp.float32,
    )
    return (highest, totals, summed)


def merge_partial(first_state, second_state):
    highest = jnp.maximum(first_state[0], second_state[0])
    first_scale = jnp.exp(first_state[0] - highest)
    second_scale = jnp.exp(second_state[0] - highest)
    totals = first_state[1] * first_scale + second_state[1] * second_scale
    summed = first_state[2] * first_scale[..., None] + second_state[2] * second_scale[..., None]
    return (highest, totals, summed)


def body(
    hidden_in,
    queries,
    suffix_kv,
    request_ids,
    group_of_request,
    page_pool,
    page_table,
    out_proj,
    norm_gain,
    routes,
    route_gates,
    w_gate,
    w_up,
    w_down,
):
    tok_rows = queries.shape[0]
    width = queries.shape[1]
    n_exp = lax.axis_size("exp")
    pool_total = page_pool.shape[0] * n_exp
    request_count = group_of_request.shape[0]
    token_group = jnp.sum(
        (request_ids[:, None] == jnp.arange(request_count, dtype=jnp.int32)[None, :]).astype(
            jnp.int32
        )
        * group_of_request[None, :],
        axis=1,
        dtype=jnp.int32,
    )
    flat_table = page_table.reshape(-1)
    table_owner = jnp.arange(flat_table.shape[0], dtype=jnp.int32) // page_table.shape[1]
    page_group = jnp.sum(
        (flat_table[:, None] == jnp.arange(pool_total, dtype=jnp.int32)[None, :]).astype(jnp.int32)
        * table_owner[:, None],
        axis=0,
        dtype=jnp.int32,
    )
    query_heads = queries.reshape(tok_rows, H, HD)
    digits = jnp.stack([request_ids % 256 + 1, request_ids // 256]).astype(jnp.bfloat16)
    earlier_kv, earlier_digits = from_behind((suffix_kv, digits), ("req", "exp"), 1)
    keys_all = jnp.concatenate([earlier_kv, suffix_kv], axis=0)
    same_before = (earlier_digits[0][None, :] == digits[0][:, None]) & (
        earlier_digits[1][None, :] == digits[1][:, None]
    )
    positions = jnp.arange(tok_rows, dtype=jnp.int32)
    same_local = (request_ids[:, None] == request_ids[None, :]) & (
        positions[None, :] <= positions[:, None]
    )
    allowed = jnp.concatenate([same_before, same_local], axis=1)
    state = partial_attend(
        query_heads,
        keys_all[:, :width].reshape(-1, H, HD),
        keys_all[:, width:].reshape(-1, H, HD),
        allowed,
    )
    running = state
    shard_piece = lax.all_gather(page_pool, "exp", axis=0, tiled=True)
    block_total = shard_piece.shape[0] // POOL_DEV
    stacked = shard_piece.reshape(block_total, POOL_DEV * PAGE, 2 * width)

    def one_block(inner, block_index):
        owners = lax.dynamic_slice_in_dim(page_group, block_index * POOL_DEV, POOL_DEV)
        needed = jnp.any(token_group[:, None] == owners[None, :])

        def attend_block(current):
            pages = lax.dynamic_index_in_dim(stacked, block_index, 0, keepdims=False)
            allowed_pages = token_group[:, None] == jnp.repeat(owners, PAGE)[None, :]
            highest, totals, summed = partial_attend(
                query_heads,
                pages[:, :width].reshape(-1, H, HD),
                pages[:, width:].reshape(-1, H, HD),
                allowed_pages,
            )
            summed = summed.astype(jnp.bfloat16).astype(jnp.float32)
            return merge_partial(current, (highest, totals, summed))

        def keep_block(current):
            return current

        return (lax.cond(needed, attend_block, keep_block, inner), None)

    running, unused = lax.scan(one_block, running, jnp.arange(block_total, dtype=jnp.int32))
    state = running
    attended = (state[2] / state[1][..., None]).reshape(tok_rows, width).astype(jnp.bfloat16)
    mixed = (
        hidden_in.astype(jnp.float32)
        + jnp.dot(attended, out_proj, preferred_element_type=jnp.float32)
    ).astype(jnp.bfloat16)
    wide = mixed.astype(jnp.float32)
    mean_square = jnp.mean(wide * wide, axis=-1, keepdims=True)
    normed = (wide * lax.rsqrt(mean_square + 1e-06) * norm_gain).astype(jnp.bfloat16)
    per_device = w_gate.shape[0]
    n_experts = per_device * n_exp
    top_count = routes.shape[1]
    capacity = (5 * tok_rows * top_count + 4 * n_experts - 1) // (4 * n_experts)
    flat_routes = routes.reshape(-1)
    hits = (flat_routes[:, None] == jnp.arange(n_experts, dtype=jnp.int32)[None, :]).astype(
        jnp.int32
    )
    ranks = jnp.cumsum(hits, axis=0, dtype=jnp.int32) - 1
    slots = jnp.sum(hits * ranks, axis=1, dtype=jnp.int32)
    position = flat_routes * capacity + slots
    cells = n_experts * capacity
    dispatch_map = (position[None, :] == jnp.arange(cells, dtype=jnp.int32)[:, None]).astype(
        jnp.bfloat16
    )
    dispatch_map = jnp.sum(dispatch_map.reshape(cells, tok_rows, top_count), axis=2)
    outgoing = jnp.dot(dispatch_map, normed, preferred_element_type=jnp.float32).astype(
        jnp.bfloat16
    )
    outgoing = outgoing.reshape(n_exp, per_device, capacity, width)
    arrived = lax.all_to_all(outgoing, "exp", split_axis=0, concat_axis=0, tiled=True)
    gate_h = jnp.einsum("sxcd,xdf->sxcf", arrived, w_gate, preferred_element_type=jnp.float32)
    up_h = jnp.einsum("sxcd,xdf->sxcf", arrived, w_up, preferred_element_type=jnp.float32)
    activ = (jax.nn.gelu(gate_h, approximate=True) * up_h).astype(jnp.bfloat16)
    finished = jnp.einsum(
        "sxcf,xfd->sxcd", activ, w_down, preferred_element_type=jnp.float32
    ).astype(jnp.bfloat16)
    arrived_back = lax.all_to_all(finished, "exp", split_axis=0, concat_axis=0, tiled=True)
    arrived_back = arrived_back.reshape(cells, width)
    picked = jnp.take(arrived_back, position, axis=0).reshape(tok_rows, top_count, width)
    layer_out = (
        wide + jnp.sum(route_gates[..., None] * picked.astype(jnp.float32), axis=1)
    ).astype(jnp.bfloat16)
    return (mixed, layer_out)


def solution(mesh):
    placed = (
        P(("req", "exp"), None),
        P(("req", "exp"), None),
        P(("req", "exp"), None),
        P(("req", "exp")),
        P(),
        P("exp", None, None),
        P(),
        P(),
        P(),
        P(("req", "exp"), None),
        P(("req", "exp"), None),
        P("exp", None, None),
        P("exp", None, None),
        P("exp", None, None),
    )
    return jax.shard_map(
        body,
        mesh=mesh,
        in_specs=placed,
        out_specs=(P(("req", "exp"), None), P(("req", "exp"), None)),
        check_vma=False,
    )
```

profile of v0, /device:TPU:0, one launch (start us, length us, event | category | flops | bytes accessed | tf_op | source)
XLA Modules:
  0.0 263.3 jit_solution(8827565197113859758)
XLA Ops:
  8.6 2.4 collective-permute-start
  11.0 4.5 %collective-permute-start.1 = (bf16[128,2048]{1,0:T(8,128)(2,1)}, bf16[128,2048]{1,0:T(8,128)(2,1)S(1)}, u32[]{:S(2)}, u32[]{:S(2)}) collective-permute-start(bf16[128,2048]{1,0:T(8,128)(2,1)} %param.20), channel_id=1, source_target_pairs={{0,1},{1,2},{2,3},{3,4},{4,5},{5,6},{6,7},{7,8},{8,9},{9,10},{10,1... | collective-permute-start | bytes 1572872 | tf_op jit(solution)/shard_map/ppermute | solution.py:20
  26.0 76.5 %all-gather.2.cloned.1.call-done = bf16[32,128,2048]{2,1,0:T(8,128)(2,1)} async-done(((bf16[4,128,2048]{2,1,0:T(8,128)(2,1)}), bf16[32,128,2048]{2,1,0:T(8,128)(2,1)}) %all-gather.2.cloned.1.call-update) | async-done | bytes 16777232 | tf_op jit(solution)/shard_map/all_gather | solution.py:106
  102.5 21.6 %copy.64 = bf16[8,512,2048]{1,2,0:T(8,128)(2,1)} copy(bf16[8,512,2048]{2,1,0:T(8,128)(2,1)} %bitcast.154) | data formatting | bytes 33554432 | tf_op jit(solution)/shard_map/while | solution.py:131
  124.1 66.2 %while.14 = (s32[]{:T(128)}, f32[128,16]{0,1:T(8,128)S(1)}, f32[128,16]{0,1:T(8,128)S(1)}, f32[128,16,64]{0,2,1:T(8,128)S(1)}, s32[128]{0:T(128)S(1)}, /*index=5...) while((s32[]{:T(128)}, f32[128,16]{0,1:T(8,128)S(1)}, ...), condition=%wide.region_10.11_spmd, body=%wide.region_4.10_spmd.sunk | while | flops 282797056 | bytes 24761768 | solution.py:131
  126.7 7.5 %conditional.2 = ((f32[128,16]{0,1:T(8,128)S(1)}, f32[128,16]{0,1:T(8,128)S(1)}, f32[128,16,64]{0,2,1:T(8,128)S(1)})) conditional(s32[]{:T(128)} %convert_element_type.156, (f32[128,16]{0,1:T(8,128)S(1)}, f32[128,16]{0,1:T(8,128)S(1)}, f32[128,16,64]{0,2,1:T(8,128)S(1)}) %tuple.47, (s32[128]{0:T(128)S(1)}, s32[4]{0:T(128)S(1)}, s32[]{:T(128)}, ...), branch_computations={%region_6.6_spmd, %region_7.9_spmd} | conditional | flops 282796032 | bytes 24760918 | solution.py:129
  128.9 1.7 dynamic-slice_bitcast_fusion
  132.8 1.5 fusion.18
  136.9 7.5 %conditional.2 = ((f32[128,16]{0,1:T(8,128)S(1)}, f32[128,16]{0,1:T(8,128)S(1)}, f32[128,16,64]{0,2,1:T(8,128)S(1)})) conditional(s32[]{:T(128)} %convert_element_type.156, (f32[128,16]{0,1:T(8,128)S(1)}, f32[128,16]{0,1:T(8,128)S(1)}, f32[128,16,64]{0,2,1:T(8,128)S(1)}) %tuple.47, (s32[128]{0:T(128)S(1)}, s32[4]{0:T(128)S(1)}, s32[]{:T(128)}, ...), branch_computations={%region_6.6_spmd, %region_7.9_spmd} | conditional | flops 282796032 | bytes 24760918 | solution.py:129
  139.0 1.7 dynamic-slice_bitcast_fusion
  147.0 7.5 %conditional.2 = ((f32[128,16]{0,1:T(8,128)S(1)}, f32[128,16]{0,1:T(8,128)S(1)}, f32[128,16,64]{0,2,1:T(8,128)S(1)})) conditional(s32[]{:T(128)} %convert_element_type.156, (f32[128,16]{0,1:T(8,128)S(1)}, f32[128,16]{0,1:T(8,128)S(1)}, f32[128,16,64]{0,2,1:T(8,128)S(1)}) %tuple.47, (s32[128]{0:T(128)S(1)}, s32[4]{0:T(128)S(1)}, s32[]{:T(128)}, ...), branch_computations={%region_6.6_spmd, %region_7.9_spmd} | conditional | flops 282796032 | bytes 24760918 | solution.py:129
  149.2 1.7 dynamic-slice_bitcast_fusion
  157.2 7.5 %conditional.2 = ((f32[128,16]{0,1:T(8,128)S(1)}, f32[128,16]{0,1:T(8,128)S(1)}, f32[128,16,64]{0,2,1:T(8,128)S(1)})) conditional(s32[]{:T(128)} %convert_element_type.156, (f32[128,16]{0,1:T(8,128)S(1)}, f32[128,16]{0,1:T(8,128)S(1)}, f32[128,16,64]{0,2,1:T(8,128)S(1)}) %tuple.47, (s32[128]{0:T(128)S(1)}, s32[4]{0:T(128)S(1)}, s32[]{:T(128)}, ...), branch_computations={%region_6.6_spmd, %region_7.9_spmd} | conditional | flops 282796032 | bytes 24760918 | solution.py:129
  159.3 1.7 dynamic-slice_bitcast_fusion
  172.6 7.5 %conditional.2 = ((f32[128,16]{0,1:T(8,128)S(1)}, f32[128,16]{0,1:T(8,128)S(1)}, f32[128,16,64]{0,2,1:T(8,128)S(1)})) conditional(s32[]{:T(128)} %convert_element_type.156, (f32[128,16]{0,1:T(8,128)S(1)}, f32[128,16]{0,1:T(8,128)S(1)}, f32[128,16,64]{0,2,1:T(8,128)S(1)}) %tuple.47, (s32[128]{0:T(128)S(1)}, s32[4]{0:T(128)S(1)}, s32[]{:T(128)}, ...), branch_computations={%region_6.6_spmd, %region_7.9_spmd} | conditional | flops 282796032 | bytes 24760918 | solution.py:129
  174.7 1.7 dynamic-slice_bitcast_fusion
  182.7 7.5 %conditional.2 = ((f32[128,16]{0,1:T(8,128)S(1)}, f32[128,16]{0,1:T(8,128)S(1)}, f32[128,16,64]{0,2,1:T(8,128)S(1)})) conditional(s32[]{:T(128)} %convert_element_type.156, (f32[128,16]{0,1:T(8,128)S(1)}, f32[128,16]{0,1:T(8,128)S(1)}, f32[128,16,64]{0,2,1:T(8,128)S(1)}) %tuple.47, (s32[128]{0:T(128)S(1)}, s32[4]{0:T(128)S(1)}, s32[]{:T(128)}, ...), branch_computations={%region_6.6_spmd, %region_7.9_spmd} | conditional | flops 282796032 | bytes 24760918 | solution.py:129
  184.9 1.7 dynamic-slice_bitcast_fusion
  191.4 28.8 %all_to_all.10 = bf16[8,1,40,1024]{3,2,1,0:T(8,128)(2,1)S(1)} all-to-all(bf16[8,1,40,1024]{3,2,1,0:T(8,128)(2,1)S(1)} %bitcast.157), channel_id=1, replica_groups=mesh['req'=4,'exp'=8] {'exp'}, dimensions={0} | all-to-all | bytes 1310720 | tf_op jit(solution)/shard_map/all_to_all | solution.py:161
  220.2 6.6 %fusion.51 = f32[8,1,40,2816]{3,2,0,1:T(8,128)} fusion(bf16[1,1024,2816]{2,1,0:T(8,128)(2,1)} %param.29, bf16[8,1,40,1024]{3,2,1,0:T(8,128)(2,1)S(1)} %all_to_all.10), kind=kOutput, calls=%fused_computation.41 | convolution fusion | flops 1852702720 | bytes 10027008 | tf_op jit(solution)/shard_map/sxcd,xdf->sxcf/dot_general | solution.py:162
  226.8 10.1 %fusion.60 = bf16[8,1,40,1024]{3,2,1,0:T(8,128)(2,1)} fusion(bf16[1,2816,1024]{2,1,0:T(8,128)(2,1)} %param.31, f32[8,1,40,2816]{3,2,0,1:T(8,128)} %fusion.51, bf16[1,1024,2816]{2,1,0:T(8,128)(2,1)} %param.30, bf16[8,1,40,1024]{3,2,1,0:T(8,128)(2,1)S(1)} %all_to_all.10), kind=kOutput, calls=%fused_computation.49 | convolution fusion | flops 3693117440 | bytes 16449536 | tf_op jit(solution)/shard_map/sxcf,xfd->sxcd/dot_general | solution.py:165
  236.9 3.5 %all-to-all-start.1 = ((bf16[8,1,40,1024]{3,2,1,0:T(8,128)(2,1)}), bf16[8,1,40,1024]{3,2,1,0:T(8,128)(2,1)S(1)}, u32[]{:S(2)}, u32[]{:S(2)}) async-start(bf16[8,1,40,1024]{3,2,1,0:T(8,128)(2,1)} %fusion.60), calls=%async_computation.1 | async-start | bytes 1310720 | tf_op jit(solution)/shard_map/all_to_all | solution.py:168
  242.3 9.3 %all-to-all-done.1 = bf16[8,1,40,1024]{3,2,1,0:T(8,128)(2,1)S(1)} async-done(((bf16[8,1,40,1024]{3,2,1,0:T(8,128)(2,1)}), bf16[8,1,40,1024]{3,2,1,0:T(8,128)(2,1)S(1)}, u32[]{:S(2)}, u32[]{:S(2)}) %all-to-all-start.1) | async-done | bytes 655392 | tf_op jit(solution)/shard_map/all_to_all | solution.py:168
  253.1 2.5 multiply_reduce_fusion
  (135 shorter events, 49.2 us)
Async XLA Ops:
  7.2 183.2 %copy-start = (bf16[1024,1024]{1,0:T(8,128)(2,1)S(1)}, bf16[1024,1024]{1,0:T(8,128)(2,1)}, u32[]{:S(2)}) copy-start(bf16[1024,1024]{1,0:T(8,128)(2,1)} %param.25) | copy-start | bytes 6291460
  7.2 15.7 %copy-start.2 = (bf16[128,2048]{1,0:T(8,128)(2,1)S(1)}, bf16[128,2048]{1,0:T(8,128)(2,1)}, u32[]{:S(2)}) copy-start(bf16[128,2048]{1,0:T(8,128)(2,1)} %param.20) | copy-start | bytes 1572868
  7.2 95.3 %all-gather.2.cloned.1.call-start = ((), (), s32[]{:S(2)}) async-start(), calls=%async_computation.2 | async-start | bytes 18874368 | tf_op jit(solution)/shard_map/all_gather | solution.py:106
  8.6 13.3 %collective-permute-start = (bf16[2,128]{1,0:T(2,128)(2,1)S(1)}, bf16[2,128]{1,0:T(2,128)(2,1)S(1)}, u32[]{:S(2)}, u32[]{:S(2)}) collective-permute-start(bf16[2,128]{1,0:T(2,128)(2,1)S(1)} %pad_maximum_fusion), channel_id=1, source_target_pairs={{0,1},{1,2},{2,3},{3,4},{4,5},{5,6},{6,7},{7,8},{8,9},{9,10},{10,1... | collective-permute-start | bytes 1544 | tf_op jit(solution)/shard_map/ppermute | solution.py:20
  11.0 11.8 %collective-permute-start.1 = (bf16[128,2048]{1,0:T(8,128)(2,1)}, bf16[128,2048]{1,0:T(8,128)(2,1)S(1)}, u32[]{:S(2)}, u32[]{:S(2)}) collective-permute-start(bf16[128,2048]{1,0:T(8,128)(2,1)} %param.20), channel_id=1, source_target_pairs={{0,1},{1,2},{2,3},{3,4},{4,5},{5,6},{6,7},{7,8},{8,9},{9,10},{10,1... | collective-permute-start | bytes 1572872 | tf_op jit(solution)/shard_map/ppermute | solution.py:20
  24.2 1.1 copy-start.3
  124.1 66.3 %copy-start.4 = (bf16[128,1024]{1,0:T(8,128)(2,1)S(1)}, bf16[128,1024]{1,0:T(8,128)(2,1)}, u32[]{:S(2)}) copy-start(bf16[128,1024]{1,0:T(8,128)(2,1)} %param.18) | copy-start | bytes 786436
  190.3 0.7 copy-start.6
  190.9 64.7 %copy-start.1 = (bf16[128,1024]{1,0:T(8,128)(2,1)}, bf16[128,1024]{1,0:T(8,128)(2,1)S(1)}, u32[]{:S(2)}) copy-start(bf16[128,1024]{1,0:T(8,128)(2,1)S(1)} %get-tuple-element.158) | copy-start | bytes 786436
  226.8 13.7 %copy-start.5 = (s32[128,2]{0,1:T(2,128)S(1)}, s32[128,2]{0,1:T(2,128)}, u32[]{:S(2)}) copy-start(s32[128,2]{0,1:T(2,128)} %param.27) | copy-start | bytes 3076
  226.8 14.0 %copy-start.7 = (pred[128,2]{0,1:T(4,128)(4,1)S(1)}, pred[128,2]{0,1:T(4,128)(4,1)}, u32[]{:S(2)}) copy-start(pred[128,2]{0,1:T(4,128)(4,1)} %get-tuple-element.143) | copy-start | bytes 772
  226.8 14.1 %copy-start.8 = (f32[128,2]{0,1:T(2,128)S(1)}, f32[128,2]{0,1:T(2,128)}, u32[]{:S(2)}) copy-start(f32[128,2]{0,1:T(2,128)} %param.28) | copy-start | bytes 3076
  236.9 14.6 %all-to-all-start.1 = ((bf16[8,1,40,1024]{3,2,1,0:T(8,128)(2,1)}), bf16[8,1,40,1024]{3,2,1,0:T(8,128)(2,1)S(1)}, u32[]{:S(2)}, u32[]{:S(2)}) async-start(bf16[8,1,40,1024]{3,2,1,0:T(8,128)(2,1)} %fusion.60), calls=%async_computation.1 | async-start | bytes 1310720 | tf_op jit(solution)/shard_map/all_to_all | solution.py:168
Sparse Core Ops, SparseCore 0:
  9.9 92.5 all-gather.1
where the time goes:
time: 265 us; the launch traced here: 263 us
  waiting for transfers between devices  86.5 us (33%)
  local copies, waits for them, and re-layouts  46 us (17%)
  matrix products  33.8 us (13%)
  blocking collectives  28.8 us (11%)
  loops' own time  22 us (8%)
  other arithmetic  21.4 us (8%)
  between operations  14.3 us (5%)
  starting transfers between devices  10.5 us (4%)
    all_gather x1, waiting for transfers between devices, body(): shard_piece = lax.all_gather(page_pool, 'exp', axis=0, tiled=True)  76.5 us
    all_to_all x1, blocking collectives, body(): lax.all_to_all(outgoing, 'exp', split_axis=0, concat_axis=0, tiled=True)  28.8 us
    while x1, local copies, waits for them, and re-layouts, body(): lax.scan(one_block, running, jnp.arange(block_total, dtype=jnp.int32))  21.6 us
    another operation x8, loops' own time, one_block(): return (lax.cond(needed, attend_block, keep_block, inner), None)  12 us
    squeeze x6, local copies, waits for them, and re-layouts, attend_block(): pages = lax.dynamic_index_in_dim(stacked, block_index, 0, keepdims=False)  10.4 us
    dot_general x1, matrix products, body(): jnp.einsum('sxcf,xfd->sxcd', activ, w_down, preferred_element_type=jnp.fl...  10.1 us
    another operation x1, loops' own time, body(): lax.scan(one_block, running, jnp.arange(block_total, dtype=jnp.int32))  9.98 us
    dot_general x7, matrix products, partial_attend(): jnp.einsum('qhk,khd->qhd', weights.astype(jnp.bfloat16), value_heads, pre...  9.41 us
  transfers between devices with their start and end apart: 4, of which 2 were waited for; matrix products, arithmetic and copies ran while one was open for 5% of the time, Pallas kernels for 0%

commit v1 on v0

v1 whole, which is shorter than its diff:
```python
import functools

import jax
import jax.numpy as jnp
from jax import lax
from jax.experimental import pallas as pl
from jax.experimental.pallas import tpu as pltpu
from jax.sharding import PartitionSpec as P

HD = 64
LANES = 128
MASKED = -1e30
MESH = pl.DeviceIdType.MESH
F32 = jnp.float32
BF16 = jnp.bfloat16
FFN_SPLIT = 1


def xor(first, second, bits):
    total = 0
    for bit in range(bits):
        a = lax.rem(lax.div(first, jnp.int32(1 << bit)), jnp.int32(2))
        b = lax.rem(lax.div(jnp.int32(second), jnp.int32(1 << bit)), jnp.int32(2))
        total = total + (a + b - 2 * a * b) * (1 << bit)
    return total


def dot(a, b, contract=(1, 0)):
    return lax.dot_general(
        a, b, (((contract[0],), (contract[1],)), ((), ())), preferred_element_type=F32
    )


def iota(shape, dim):
    return lax.broadcasted_iota(jnp.int32, shape, dim)


def stack_heads(pair):
    wide = pair.astype(F32) * (1.0 / 8.0)
    low = iota(wide.shape, 1) < HD
    return jnp.concatenate(
        [jnp.where(low, wide, 0.0), jnp.where(low, 0.0, wide)], axis=0
    ).astype(BF16)


def soft_pair(scores, values):
    highest = jnp.max(scores, axis=1, keepdims=True)
    weights = jnp.exp(scores - highest).astype(BF16)
    both = dot(weights, jnp.concatenate([values, jnp.ones_like(values)], axis=1))
    totals = both[:, LANES:]
    return both[:, :LANES] / totals, highest + jnp.log(totals)


def kernel(
    n_req, n_exp, cap,
    hidden, queries, kv, ids, groups, pool, table, wo, gain, routes, gates, wg, wu, wd,
    mixed_out, layer_out,
    q_v, tg_v, pages_v, kaug_v, kv_v, kvp_v, ids_v, idp_v, hid_v, wo_v, wg_v, wu_v, wd_v,
    osend_v, orecv_v, lsend_v, lrecv_v, sufo_v, sufl_v, map_v, mix_v,
    disp_v, arr_v, act_v, fin_v, back_v,
    loc_sem, q_s, q_r, tg_s, tg_r, o_s, o_r, l_s, l_r, d_s, d_r, b_s, b_r, one_s, one_r,
):
    n_chip = n_exp // 2
    bits = (n_exp - 1).bit_length()
    rows, width = hid_v.shape
    pairs = width // LANES
    heads = width // HD
    per_dev = pool.shape[0]
    page = pool.shape[1]
    me_r = lax.axis_index("req")
    me = lax.axis_index("exp")
    total = n_req * n_exp
    flat = me_r * n_exp + me
    after = lax.rem(flat + 1, total)
    before = lax.rem(flat + total - 1, total)
    nxt = (lax.div(after, n_exp), lax.rem(after, n_exp))
    prv = (lax.div(before, n_exp), lax.rem(before, n_exp))
    peers = [None] + [xor(me, k, bits) for k in range(1, n_exp)]
    mate = peers[1]

    def local(src, dst, i):
        return pltpu.make_async_copy(src, dst, loc_sem.at[i])

    c_q = local(queries, q_v.at[0], 0)
    c_pages = local(pool, pages_v.at[pl.ds(0, per_dev)], 1)
    c_kv = local(kv, kv_v, 2)
    c_hid = local(hidden, hid_v, 3)
    c_wo = local(wo, wo_v, 4)
    c_wg = local(wg.at[0], wg_v, 5)
    c_wu = local(wu.at[0], wu_v, 6)
    c_wd = local(wd.at[0], wd_v, 7)
    c_q.start()
    c_pages.start()

    barrier = pltpu.get_barrier_semaphore()
    for peer in peers[1:]:
        pl.semaphore_signal(barrier, inc=1, device_id=(me_r, peer), device_id_type=MESH)
    pl.semaphore_signal(barrier, inc=1, device_id=nxt, device_id_type=MESH)
    pl.semaphore_signal(barrier, inc=1, device_id=prv, device_id_type=MESH)

    own_ids = ids[...]
    ids_v[...] = jnp.broadcast_to(own_ids, ids_v.shape)
    ids_tile = jnp.broadcast_to(own_ids, (8, rows))

    def add_group(r, acc):
        return jnp.where(ids_tile == r, groups[r], acc)

    tg_v[0] = lax.fori_loop(
        0, groups.shape[0], add_group, jnp.zeros((8, rows), jnp.int32), unroll=8
    )

    pl.semaphore_wait(barrier, n_exp + 1)

    def remote(src, dst, send, recv, device):
        return pltpu.make_async_remote_copy(
            src_ref=src, dst_ref=dst, send_sem=send, recv_sem=recv,
            device_id=device, device_id_type=MESH,
        )

    def chip_peer(k):
        return (me_r, xor(me, 2 * k, bits))

    def send_q(k):
        return remote(queries, q_v.at[k], q_s.at[k], q_r.at[k], chip_peer(k))

    def send_tg(k):
        return remote(tg_v.at[0], tg_v.at[k], tg_s.at[k], tg_r.at[k], chip_peer(k))

    def send_o(k):
        return remote(osend_v.at[k], orecv_v.at[k], o_s.at[k], o_r.at[k], chip_peer(k))

    def send_l(k):
        return remote(lsend_v.at[k], lrecv_v.at[k], l_s.at[k], l_r.at[k], chip_peer(k))

    s_pages = remote(
        pool, pages_v.at[pl.ds(per_dev, per_dev)], one_s.at[0], one_r.at[0], (me_r, mate)
    )
    s_kv = remote(kv, kvp_v, one_s.at[1], one_r.at[1], nxt)
    s_id = remote(ids_v, idp_v, one_s.at[2], one_r.at[2], nxt)

    s_pages.start()
    for k in range(1, n_chip):
        send_tg(k).start()
        send_q(k).start()
    s_id.start()
    s_kv.start()
    c_kv.start()
    c_hid.start()
    c_wo.start()
    c_wg.start()
    c_wu.start()
    c_wd.start()

    sub = iota((8, LANES), 0)
    n_slot = 2 * per_dev
    page_ids = jnp.where(sub < per_dev, me * per_dev + sub, mate * per_dev + sub - per_dev)
    owner = jnp.zeros((8, LANES), jnp.int32)
    for g in range(table.shape[0]):
        for i in range(table.shape[1]):
            owner = jnp.where(page_ids == table[g, i], g, owner)
    lane_page = iota((page, LANES), 1)
    for s in range(n_slot):
        kaug_v[s] = jnp.where(owner[s : s + 1, :] == lane_page, 1.0, 0.0).astype(BF16)

    lane = iota((rows, LANES), 1)
    gathered = jnp.where(
        lane == 0,
        routes[:, 0:1].astype(F32),
        jnp.where(
            lane == 1,
            routes[:, 1:2].astype(F32),
            jnp.where(lane == 2, gates[:, 0:1], gates[:, 1:2]),
        ),
    )
    turned = gathered.T
    r0, r1, g0, g1 = (turned[i : i + 1, :] for i in range(4))
    sub_e = iota((n_exp, rows), 0)
    experts = jnp.broadcast_to(me, (n_exp, rows))
    for k in range(1, n_exp):
        experts = jnp.where(sub_e == k, peers[k], experts)
    experts = experts.astype(F32)
    first = experts == r0
    second = experts == r1
    hit = jnp.where(first | second, 1.0, 0.0)
    gate = jnp.where(first, g0, g1)
    earlier = jnp.where(iota((rows, rows), 0) < iota((rows, rows), 1), 1.0, 0.0).astype(BF16)
    rank = dot(hit.astype(BF16), earlier)
    rank = jnp.where(hit > 0.0, rank, -1.0)
    slot = iota((cap, rows), 0).astype(F32)
    for k in range(n_exp):
        taken = jnp.where(rank[k : k + 1, :] == slot, 1.0, 0.0)
        weight = taken * gate[k : k + 1, :]
        high = weight.astype(BF16)
        at = pl.ds(k * cap, cap)
        map_v[0, at, :] = taken.astype(BF16)
        map_v[1, at, :] = high
        map_v[2, at, :] = (weight - high.astype(F32)).astype(BF16)

    c_q.wait()
    c_pages.wait()
    s_pages.wait_recv()

    def one_chip(k, carry):
        @pl.when(k > 0)
        def _():
            send_tg(k).wait_recv()
            send_q(k).wait_recv()

        group_col = jnp.broadcast_to(tg_v[k, 0:1, :].astype(F32), (LANES, rows)).T
        aug = jnp.where(group_col == lane.astype(F32), 0.0, MASKED)
        aug = jnp.concatenate([aug, aug], axis=0).astype(BF16)
        kaug = kaug_v[...].reshape(n_slot * page, LANES)

        def one_pair(p, logs):
            at = pl.ds(pl.multiple_of(p * LANES, LANES), LANES)
            vat = pl.ds(pl.multiple_of(width + p * LANES, LANES), LANES)
            left = jnp.concatenate([stack_heads(q_v[k, :, at]), aug], axis=1)
            keys = pages_v[:, :, at].reshape(n_slot * page, LANES)
            scores = dot(left, jnp.concatenate([keys, kaug], axis=1), (1, 1))
            values = pages_v[:, :, vat].reshape(n_slot * page, LANES)
            out, lse = soft_pair(scores, values)
            osend_v[k, :, at] = jnp.where(lane < HD, out[:rows], out[rows:]).astype(BF16)
            return jnp.where(
                lane == 2 * p, lse[:rows], jnp.where(lane == 2 * p + 1, lse[rows:], logs)
            )

        logs = lax.fori_loop(0, pairs, one_pair, jnp.zeros((rows, LANES), F32))
        lsend_v[k] = logs.T[:heads]

        @pl.when(k > 0)
        def _():
            send_o(k).start()
            send_l(k).start()

        return carry

    lax.fori_loop(0, n_chip, one_chip, 0)

    c_kv.wait()
    s_id.wait_recv()
    s_kv.wait_recv()
    id_col = jnp.broadcast_to(own_ids.astype(F32), (LANES, rows)).T
    past = jnp.where(flat > 0, idp_v[0:1, :].astype(F32), -1.0)
    bias_before = jnp.where(id_col == past, 0.0, MASKED)
    bias_own = jnp.where(
        (id_col == own_ids.astype(F32)) & (lane <= iota((rows, LANES), 0)), 0.0, MASKED
    )
    bias = jnp.concatenate([bias_before, bias_own], axis=1)

    def suffix_pair(p, logs):
        at = pl.ds(pl.multiple_of(p * LANES, LANES), LANES)
        vat = pl.ds(pl.multiple_of(width + p * LANES, LANES), LANES)
        keys = jnp.concatenate([kvp_v[:, at], kv_v[:, at]], axis=0)
        values = jnp.concatenate([kvp_v[:, vat], kv_v[:, vat]], axis=0)
        scores = dot(stack_heads(q_v[0, :, at]), keys, (1, 1))
        scores = scores + jnp.concatenate([bias, bias], axis=0)
        out, lse = soft_pair(scores, values)
        sufo_v[:, at] = jnp.where(lane < HD, out[:rows], out[rows:])
        return jnp.where(
            lane == 2 * p, lse[:rows], jnp.where(lane == 2 * p + 1, lse[rows:], logs)
        )

    suffix_logs = lax.fori_loop(0, pairs, suffix_pair, jnp.zeros((rows, LANES), F32))

    for k in range(1, n_chip):
        send_l(k).wait_recv()
        send_o(k).wait_recv()
    logs = [suffix_logs.T[:heads], lsend_v[0]] + [lrecv_v[k] for k in range(1, n_chip)]
    top = functools.reduce(jnp.maximum, logs)
    shares = [jnp.exp(entry - top) for entry in logs]
    below = functools.reduce(jnp.add, shares)
    spread = jnp.where(
        lax.rem(iota((2 * heads, width), 0), heads) == lax.div(iota((2 * heads, width), 1), HD),
        1.0,
        0.0,
    ).astype(BF16)
    attended = None
    for j, share in enumerate(shares):
        share = share / below
        high = share.astype(BF16)
        low = (share - high.astype(F32)).astype(BF16)
        scale = dot(jnp.concatenate([high, low], axis=0), spread, (0, 0))
        if j == 0:
            part = sufo_v[...]
        elif j == 1:
            part = osend_v[0].astype(F32)
        else:
            part = orecv_v[j - 1].astype(F32)
        attended = scale * part if attended is None else attended + scale * part
    c_wo.wait()
    c_hid.wait()
    mixed = (hid_v[...].astype(F32) + dot(attended.astype(BF16), wo_v[...])).astype(BF16)
    mixed_out[...] = mixed
    wide = mixed.astype(F32)
    mean_square = jnp.mean(wide * wide, axis=1, keepdims=True)
    mix_v[...] = (wide * lax.rsqrt(mean_square + 1e-6) * gain[...]).astype(BF16)

    def send_d(k):
        return remote(disp_v.at[k], arr_v.at[k], d_s.at[k], d_r.at[k], (me_r, peers[k]))

    def send_b(k):
        return remote(fin_v.at[k], back_v.at[k], b_s.at[k], b_r.at[k], (me_r, peers[k]))

    for k in reversed(range(n_exp)):
        out = dot(map_v[0, pl.ds(k * cap, cap), :], mix_v[...]).astype(BF16)
        if k > 0:
            disp_v[k] = out
            send_d(k).start()
        else:
            arr_v[0] = out

    tile = 256
    part = n_exp // FFN_SPLIT
    for half in range(FFN_SPLIT):
        slots = pl.ds(half * part, part)
        for k in range(half * part, (half + 1) * part):
            if k > 0:
                send_d(k).wait_recv()
        if half == 0:
            c_wg.wait()
            c_wu.wait()

        @pl.loop(0, wg_v.shape[1] // tile)
        def _(i):
            at = pl.ds(pl.multiple_of(i * tile, tile), tile)
            x = arr_v[slots].reshape(part * cap, width)
            gate_h = dot(x, wg_v[:, at])
            up_h = dot(x, wu_v[:, at])
            act_v[:, at] = (jax.nn.gelu(gate_h, approximate=True) * up_h).astype(BF16)

        if half == 0:
            c_wd.wait()

        @pl.loop(0, width // tile)
        def _(i):
            at = pl.ds(pl.multiple_of(i * tile, tile), tile)
            y = dot(act_v[...], wd_v[:, at]).astype(BF16)
            fin_v[slots, :, at] = y.reshape(part, cap, tile)

        for k in reversed(range(half * part, (half + 1) * part)):
            if k > 0:
                send_b(k).start()
            else:
                back_v[0] = fin_v[0]

    for k in range(1, n_exp):
        send_b(k).wait_recv()
    back = back_v[...].reshape(n_exp * cap, width)
    routed = dot(map_v[1], back, (0, 0)) + dot(map_v[2], back, (0, 0))
    layer_out[...] = (mixed_out[...].astype(F32) + routed).astype(BF16)

    s_pages.wait_send()
    s_kv.wait_send()
    s_id.wait_send()
    for k in range(1, n_chip):
        send_q(k).wait_send()
        send_tg(k).wait_send()
        send_o(k).wait_send()
        send_l(k).wait_send()
    for k in range(1, n_exp):
        send_d(k).wait_send()
        send_b(k).wait_send()


def body(
    n_req, n_exp,
    hidden_in, queries, suffix_kv, request_ids, group_of_request, page_pool, page_table,
    out_proj, norm_gain, routes, route_gates, w_gate, w_up, w_down,
):
    rows, width = queries.shape
    ff = w_gate.shape[2]
    per_dev, page = page_pool.shape[0], page_pool.shape[1]
    top_count = routes.shape[1]
    cap = (5 * rows * top_count + 4 * n_exp - 1) // (4 * n_exp)
    cap = (cap + 15) // 16 * 16
    n_chip = n_exp // 2
    heads = width // HD
    hbm = pl.BlockSpec(memory_space=pl.ANY)
    vmem = pl.BlockSpec(memory_space=pltpu.VMEM)
    smem = pl.BlockSpec(memory_space=pltpu.SMEM)
    dma = pltpu.SemaphoreType.DMA
    v = pltpu.VMEM
    out = jax.ShapeDtypeStruct((rows, width), BF16)
    part_rows = n_exp // FFN_SPLIT * cap
    return pl.pallas_call(
        functools.partial(kernel, n_req, n_exp, cap),
        out_shape=(out, out),
        in_specs=[
            hbm, hbm, hbm, vmem, smem, hbm, smem, hbm, vmem, vmem, vmem, hbm, hbm, hbm,
        ],
        out_specs=(vmem, vmem),
        scratch_shapes=[
            v((n_chip, rows, width), BF16),
            v((n_chip, 8, rows), jnp.int32),
            v((2 * per_dev, page, 2 * width), BF16),
            v((2 * per_dev, page, LANES), BF16),
            v((rows, 2 * width), BF16),
            v((rows, 2 * width), BF16),
            v((8, rows), jnp.int32),
            v((8, rows), jnp.int32),
            v((rows, width), BF16),
            v((width, width), BF16),
            v((width, ff), BF16),
            v((width, ff), BF16),
            v((ff, width), BF16),
            v((n_chip, rows, width), BF16),
            v((n_chip, rows, width), BF16),
            v((n_chip, heads, rows), F32),
            v((n_chip, heads, rows), F32),
            v((rows, width), F32),
            v((heads, rows), F32),
            v((3, n_exp * cap, rows), BF16),
            v((rows, width), BF16),
            v((n_exp, cap, width), BF16),
            v((n_exp, cap, width), BF16),
            v((part_rows, ff), BF16),
            v((n_exp, cap, width), BF16),
            v((n_exp, cap, width), BF16),
            dma((8,)),
            dma((n_chip,)), dma((n_chip,)),
            dma((n_chip,)), dma((n_chip,)),
            dma((n_chip,)), dma((n_chip,)),
            dma((n_chip,)), dma((n_chip,)),
            dma((n_exp,)), dma((n_exp,)),
            dma((n_exp,)), dma((n_exp,)),
            dma((3,)), dma((3,)),
        ],
        compiler_params=pltpu.CompilerParams(
            collective_id=0, has_side_effects=True, vmem_limit_bytes=58 * 1024 * 1024
        ),
        name="layer",
    )(
        hidden_in, queries, suffix_kv, request_ids.reshape(1, rows), group_of_request,
        page_pool, page_table, out_proj, norm_gain.reshape(1, width), routes, route_gates,
        w_gate, w_up, w_down,
    )


def solution(mesh):
    tokens = P(("req", "exp"), None)
    placed = (
        tokens, tokens, tokens, P(("req", "exp")), P(), P("exp", None, None), P(), P(), P(),
        tokens, tokens, P("exp", None, None), P("exp", None, None), P("exp", None, None),
    )
    return jax.shard_map(
        functools.partial(body, mesh.shape["req"], mesh.shape["exp"]),
        mesh=mesh,
        in_specs=placed,
        out_specs=(tokens, tokens),
        check_vma=False,
    )
```

time: 265 us -> 87.1 us (0.33)
  waiting for transfers between devices: 86.5 us -> 0 us
  Pallas kernels: 0 us -> 80.1 us
  local copies, waits for them, and re-layouts: 46 us -> 6.17 us
  matrix products: 33.8 us -> 0 us
  blocking collectives: 28.8 us -> 0 us
  loops' own time: 22 us -> 0 us
  other arithmetic: 21.4 us -> 0 us
  between operations: 14.3 us -> 0.64 us
  starting transfers between devices: 10.5 us -> 0 us
    pallas_call x0 -> x1, Pallas kernels: none -> 80.1 us  [body(): pl.pallas_call(functools.partial(kernel, n_req, n_exp, cap), out_shape=(o...]
    all_gather x1 -> x0, waiting for transfers between devices: 76.5 us -> none  [body(): shard_piece = lax.all_gather(page_pool, 'exp', axis=0, tiled=True)]
    dot_general x18 -> x0, matrix products: 33.8 us -> none  [the longest x1 10.1 us: body(): jnp.einsum('sxcf,xfd->sxcd', activ, w_down, preferred_element_type=jnp.fl...]
    all_to_all x1 -> x0, blocking collectives: 28.8 us -> none  [body(): lax.all_to_all(outgoing, 'exp', split_axis=0, concat_axis=0, tiled=True)]
    another operation x9 -> x0, loops' own time: 22 us -> none  [the longest x8 12 us: one_block(): return (lax.cond(needed, attend_block, keep_block, inner), None)]
    while x1 -> x0, local copies, waits for them, and re-layouts: 21.6 us -> none  [body(): lax.scan(one_block, running, jnp.arange(block_total, dtype=jnp.int32))]
    squeeze x6 -> x0, local copies, waits for them, and re-layouts: 10.4 us -> none  [attend_block(): pages = lax.dynamic_index_in_dim(stacked, block_index, 0, keepdims=False)]
    reduce_sum x12 -> x0, other arithmetic: 9.96 us -> none  [the longest x7 6.41 us: partial_attend(): totals = jnp.sum(weights, axis=-1)]
  transfers between devices with their start and end apart: 4 -> 0, of which waited for: 2 -> 0; matrix products, arithmetic and copies ran while one was open for 5% -> 0% of each run, Pallas kernels for 0% -> 0%
where the time goes in v1:
time: 87.1 us; the launch traced here: 86.9 us
  Pallas kernels  80.1 us (92%)
  local copies, waits for them, and re-layouts  6.17 us (7%)
    pallas_call x1, Pallas kernels, body(): pl.pallas_call(functools.partial(kernel, n_req, n_exp, cap), out_shape=(o...  80.1 us
    unnamed x4, local copies, waits for them, and re-layouts  6.17 us

profile of v1, /device:TPU:0, one launch (start us, length us, event | category | flops | bytes accessed | tf_op | source)
XLA Modules:
  0.0 86.9 jit_solution(5534422685052822180)
XLA Ops:
  0.6 1.4 %copy.16.routes = s32[128,2]{1,0:T(8,128)} copy(s32[128,2]{0,1:T(2,128)} %param.23) | data formatting | bytes 2048 | tf_op args[9]
  2.0 1.4 %copy.17.gates = f32[128,2]{1,0:T(8,128)} copy(f32[128,2]{0,1:T(2,128)} %param.24) | data formatting | bytes 2048 | tf_op args[10]
  3.5 80.1 %layer.1 = (bf16[128,1024]{1,0:T(8,128)(2,1)}, bf16[128,1024]{1,0:T(8,128)(2,1)}) custom-call(bf16[128,1024]{1,0:T(8,128)(2,1)} %hidden.1, bf16[128,1024]{1,0:T(8,128)(2,1)} %queries.1, bf16[128,2048]{1,0:T(8,128)(2,1)} %kv.1, s32[1,128]{1,0:T(1,128)} %bitcast.3, s32[64]{0:T(128)} %groups.1, bf16[4,128,2048]{2,1,0:T(8,128)(2,1)} %pool.1, s32[4,8]{1,0:T(4,128)} %table.1, ...), custom_call_target="tpu_custom_call" | custom-call | tf_op jit(solution)/shard_map/layer/pallas_call | solution.py:385
  83.5 1.7 %copy.20 = bf16[128,1024]{1,0:T(8,128)(2,1)} copy(bf16[128,1024]{1,0:T(8,128)(2,1)} %get-tuple-element.4) | data formatting | bytes 524288
  85.2 1.7 %copy.21 = bf16[128,1024]{1,0:T(8,128)(2,1)} copy(bf16[128,1024]{1,0:T(8,128)(2,1)} %get-tuple-element.5) | data formatting | bytes 524288

commit v2 on v1

--- a/solution.py
+++ b/solution.py
@@ -13,7 +13,6 @@
 MESH = pl.DeviceIdType.MESH
 F32 = jnp.float32
 BF16 = jnp.bfloat16
-FFN_SPLIT = 1
 
 
 def xor(first, second, bits):
@@ -56,7 +55,7 @@
     hidden, queries, kv, ids, groups, pool, table, wo, gain, routes, gates, wg, wu, wd,
     mixed_out, layer_out,
     q_v, tg_v, pages_v, kaug_v, kv_v, kvp_v, ids_v, idp_v, hid_v, wo_v, wg_v, wu_v, wd_v,
-    osend_v, orecv_v, lsend_v, lrecv_v, sufo_v, sufl_v, map_v, mix_v,
+    osend_v, orecv_v, lsend_v, lrecv_v, sufo_v, map_v, comb_v, x_v, mix_v,
     disp_v, arr_v, act_v, fin_v, back_v,
     loc_sem, q_s, q_r, tg_s, tg_r, o_s, o_r, l_s, l_r, d_s, d_r, b_s, b_r, one_s, one_r,
 ):
@@ -163,17 +162,8 @@
         kaug_v[s] = jnp.where(owner[s : s + 1, :] == lane_page, 1.0, 0.0).astype(BF16)
 
     lane = iota((rows, LANES), 1)
-    gathered = jnp.where(
-        lane == 0,
-        routes[:, 0:1].astype(F32),
-        jnp.where(
-            lane == 1,
-            routes[:, 1:2].astype(F32),
-            jnp.where(lane == 2, gates[:, 0:1], gates[:, 1:2]),
-        ),
-    )
-    turned = gathered.T
-    r0, r1, g0, g1 = (turned[i : i + 1, :] for i in range(4))
+    r0, r1 = routes[0:1, :].astype(F32), routes[1:2, :].astype(F32)
+    g0, g1 = gates[0:1, :], gates[1:2, :]
     sub_e = iota((n_exp, rows), 0)
     experts = jnp.broadcast_to(me, (n_exp, rows))
     for k in range(1, n_exp):
@@ -187,14 +177,13 @@
     rank = dot(hit.astype(BF16), earlier)
     rank = jnp.where(hit > 0.0, rank, -1.0)
     slot = iota((cap, rows), 0).astype(F32)
-    for k in range(n_exp):
-        taken = jnp.where(rank[k : k + 1, :] == slot, 1.0, 0.0)
-        weight = taken * gate[k : k + 1, :]
-        high = weight.astype(BF16)
-        at = pl.ds(k * cap, cap)
-        map_v[0, at, :] = taken.astype(BF16)
-        map_v[1, at, :] = high
-        map_v[2, at, :] = (weight - high.astype(F32)).astype(BF16)
+    taken = [jnp.where(rank[k : k + 1, :] == slot, 1.0, 0.0) for k in range(n_exp)]
+    weight = [taken[k] * gate[k : k + 1, :] for k in range(n_exp)]
+    map_v[...] = jnp.concatenate(taken, axis=0).astype(BF16)
+    weight = jnp.concatenate(weight, axis=0).T
+    high = weight.astype(BF16)
+    comb_v[pl.ds(0, rows), :] = high
+    comb_v[pl.ds(rows, rows), :] = (weight - high.astype(F32)).astype(BF16)
 
     c_q.wait()
     c_pages.wait()
@@ -224,7 +213,7 @@
                 lane == 2 * p, lse[:rows], jnp.where(lane == 2 * p + 1, lse[rows:], logs)
             )
 
-        logs = lax.fori_loop(0, pairs, one_pair, jnp.zeros((rows, LANES), F32))
+        logs = lax.fori_loop(0, pairs, one_pair, jnp.zeros((rows, LANES), F32), unroll=8)
         lsend_v[k] = logs.T[:heads]
 
         @pl.when(k > 0)
@@ -260,7 +249,7 @@
             lane == 2 * p, lse[:rows], jnp.where(lane == 2 * p + 1, lse[rows:], logs)
         )
 
-    suffix_logs = lax.fori_loop(0, pairs, suffix_pair, jnp.zeros((rows, LANES), F32))
+    suffix_logs = lax.fori_loop(0, pairs, suffix_pair, jnp.zeros((rows, LANES), F32), unroll=4)
 
     for k in range(1, n_chip):
         send_l(k).wait_recv()
@@ -274,19 +263,14 @@
         1.0,
         0.0,
     ).astype(BF16)
-    attended = None
-    for j, share in enumerate(shares):
-        share = share / below
-        high = share.astype(BF16)
-        low = (share - high.astype(F32)).astype(BF16)
-        scale = dot(jnp.concatenate([high, low], axis=0), spread, (0, 0))
-        if j == 0:
-            part = sufo_v[...]
-        elif j == 1:
-            part = osend_v[0].astype(F32)
-        else:
-            part = orecv_v[j - 1].astype(F32)
-        attended = scale * part if attended is None else attended + scale * part
+    shares = jnp.concatenate([share / below for share in shares], axis=1)
+    high = shares.astype(BF16)
+    low = (shares - high.astype(F32)).astype(BF16)
+    scales = dot(jnp.concatenate([high, low], axis=0), spread, (0, 0))
+    attended = scales[:rows] * sufo_v[...] + scales[rows : 2 * rows] * osend_v[0].astype(F32)
+    for k in range(1, n_chip):
+        at = (k + 1) * rows
+        attended = attended + scales[at : at + rows] * orecv_v[k].astype(F32)
     c_wo.wait()
     c_hid.wait()
     mixed = (hid_v[...].astype(F32) + dot(attended.astype(BF16), wo_v[...])).astype(BF16)
@@ -301,52 +285,54 @@
     def send_b(k):
         return remote(fin_v.at[k], back_v.at[k], b_s.at[k], b_r.at[k], (me_r, peers[k]))
 
-    for k in reversed(range(n_exp)):
-        out = dot(map_v[0, pl.ds(k * cap, cap), :], mix_v[...]).astype(BF16)
-        if k > 0:
-            disp_v[k] = out
-            send_d(k).start()
-        else:
-            arr_v[0] = out
-
+    half = width // 2
+
+    def fold(rows_in):
+        grid = rows_in.reshape(n_exp, cap, rows_in.shape[1])
+        cut = rows_in.shape[1] // 2
+        return jnp.concatenate([grid[:, :, :cut], grid[:, :, cut:]], axis=1).astype(BF16)
+
+    def unfold(ref):
+        grid = ref[...].astype(F32)
+        grid = jnp.concatenate([grid[:, :cap], grid[:, cap:]], axis=2)
+        return grid.reshape(n_exp * cap, width).astype(BF16)
+
+    disp_v[...] = fold(dot(map_v[...], mix_v[...]))
+    for k in reversed(range(1, n_exp)):
+        send_d(k).start()
+    arr_v[0] = disp_v[0]
+    for k in range(1, n_exp):
+        send_d(k).wait_recv()
+    x_v[...] = unfold(arr_v)
+    c_wg.wait()
+    c_wu.wait()
     tile = 256
-    part = n_exp // FFN_SPLIT
-    for half in range(FFN_SPLIT):
-        slots = pl.ds(half * part, part)
-        for k in range(half * part, (half + 1) * part):
-            if k > 0:
-                send_d(k).wait_recv()
-        if half == 0:
-            c_wg.wait()
-            c_wu.wait()
-
-        @pl.loop(0, wg_v.shape[1] // tile)
-        def _(i):
-            at = pl.ds(pl.multiple_of(i * tile, tile), tile)
-            x = arr_v[slots].reshape(part * cap, width)
-            gate_h = dot(x, wg_v[:, at])
-            up_h = dot(x, wu_v[:, at])
-            act_v[:, at] = (jax.nn.gelu(gate_h, approximate=True) * up_h).astype(BF16)
-
-        if half == 0:
-            c_wd.wait()
-
-        @pl.loop(0, width // tile)
-        def _(i):
-            at = pl.ds(pl.multiple_of(i * tile, tile), tile)
-            y = dot(act_v[...], wd_v[:, at]).astype(BF16)
-            fin_v[slots, :, at] = y.reshape(part, cap, tile)
-
-        for k in reversed(range(half * part, (half + 1) * part)):
-            if k > 0:
-                send_b(k).start()
-            else:
-                back_v[0] = fin_v[0]
+
+    @pl.loop(0, wg_v.shape[1] // tile)
+    def _(i):
+        at = pl.ds(pl.multiple_of(i * tile, tile), tile)
+        gate_h = dot(x_v[...], wg_v[:, at])
+        up_h = dot(x_v[...], wu_v[:, at])
+        act_v[:, at] = (jax.nn.gelu(gate_h, approximate=True) * up_h).astype(BF16)
+
+    c_wd.wait()
+
+    @pl.loop(0, half // tile)
+    def _(i):
+        at = pl.ds(pl.multiple_of(i * tile, tile), tile)
+        far = pl.ds(pl.multiple_of(half + i * tile, tile), tile)
+        near_y = dot(act_v[...], wd_v[:, at])
+        far_y = dot(act_v[...], wd_v[:, far])
+        fin_v[:, :, at] = fold(jnp.concatenate([near_y, far_y], axis=1))
+
+    for k in reversed(range(1, n_exp)):
+        send_b(k).start()
+    back_v[0] = fin_v[0]
 
     for k in range(1, n_exp):
         send_b(k).wait_recv()
-    back = back_v[...].reshape(n_exp * cap, width)
-    routed = dot(map_v[1], back, (0, 0)) + dot(map_v[2], back, (0, 0))
+    both = dot(comb_v[...], unfold(back_v))
+    routed = both[:rows] + both[rows:]
     layer_out[...] = (mixed_out[...].astype(F32) + routed).astype(BF16)
 
     s_pages.wait_send()
@@ -362,6 +348,15 @@
         send_b(k).wait_send()
 
 
+def hand_over(mixed, layer, mixed_out, layer_out, sem):
+    first = pltpu.make_async_copy(mixed, mixed_out, sem.at[0])
+    second = pltpu.make_async_copy(layer, layer_out, sem.at[1])
+    first.start()
+    second.start()
+    first.wait()
+    second.wait()
+
+
 def body(
     n_req, n_exp,
     hidden_in, queries, suffix_kv, request_ids, group_of_request, page_pool, page_table,
@@ -372,7 +367,7 @@
     per_dev, page = page_pool.shape[0], page_pool.shape[1]
     top_count = routes.shape[1]
     cap = (5 * rows * top_count + 4 * n_exp - 1) // (4 * n_exp)
-    cap = (cap + 15) // 16 * 16
+    cap = (cap + 7) // 8 * 8
     n_chip = n_exp // 2
     heads = width // HD
     hbm = pl.BlockSpec(memory_space=pl.ANY)
@@ -381,8 +376,7 @@
     dma = pltpu.SemaphoreType.DMA
     v = pltpu.VMEM
     out = jax.ShapeDtypeStruct((rows, width), BF16)
-    part_rows = n_exp // FFN_SPLIT * cap
-    return pl.pallas_call(
+    results = pl.pallas_call(
         functools.partial(kernel, n_req, n_exp, cap),
         out_shape=(out, out),
         in_specs=[
@@ -408,14 +402,15 @@
             v((n_chip, heads, rows), F32),
             v((n_chip, heads, rows), F32),
             v((rows, width), F32),
-            v((heads, rows), F32),
-            v((3, n_exp * cap, rows), BF16),
+            v((n_exp * cap, rows), BF16),
+            v((2 * rows, n_exp * cap), BF16),
+            v((n_exp * cap, width), BF16),
             v((rows, width), BF16),
-            v((n_exp, cap, width), BF16),
-            v((n_exp, cap, width), BF16),
-            v((part_rows, ff), BF16),
-            v((n_exp, cap, width), BF16),
-            v((n_exp, cap, width), BF16),
+            v((n_exp, 2 * cap, width // 2), BF16),
+            v((n_exp, 2 * cap, width // 2), BF16),
+            v((n_exp * cap, ff), BF16),
+            v((n_exp, 2 * cap, width // 2), BF16),
+            v((n_exp, 2 * cap, width // 2), BF16),
             dma((8,)),
             dma((n_chip,)), dma((n_chip,)),
             dma((n_chip,)), dma((n_chip,)),
@@ -431,9 +426,10 @@
         name="layer",
     )(
         hidden_in, queries, suffix_kv, request_ids.reshape(1, rows), group_of_request,
-        page_pool, page_table, out_proj, norm_gain.reshape(1, width), routes, route_gates,
+        page_pool, page_table, out_proj, norm_gain.reshape(1, width), routes.T, route_gates.T,
         w_gate, w_up, w_down,
     )
+    return results
 
 
 def solution(mesh):

time: 87.1 us -> 69.9 us (0.80)
  Pallas kernels: 80.1 us -> 65.5 us
  local copies, waits for them, and re-layouts: 6.17 us -> 3.34 us
    pallas_call x1, Pallas kernels: 80.1 us -> 65.5 us  [body(): pl.pallas_call(functools.partial(kernel, n_req, n_exp, cap), out_shape=(o...]
    unnamed x4 -> x2, local copies, waits for them, and re-layouts: 6.17 us -> 3.34 us
where the time goes in v2:
time: 69.9 us; the launch traced here: 69.5 us
  Pallas kernels  65.5 us (94%)
  local copies, waits for them, and re-layouts  3.34 us (5%)
    pallas_call x1, Pallas kernels, body(): pl.pallas_call(functools.partial(kernel, n_req, n_exp, cap), out_shape=(o...  65.5 us
    unnamed x2, local copies, waits for them, and re-layouts  3.34 us

profile of v2, /device:TPU:0, one launch (start us, length us, event | category | flops | bytes accessed | tf_op | source)
XLA Modules:
  0.0 69.5 jit_solution(2484889654698595135)
XLA Ops:
  0.6 65.5 %layer.1 = (bf16[128,1024]{1,0:T(8,128)(2,1)}, bf16[128,1024]{1,0:T(8,128)(2,1)}) custom-call(bf16[128,1024]{1,0:T(8,128)(2,1)} %hidden.1, bf16[128,1024]{1,0:T(8,128)(2,1)} %queries.1, bf16[128,2048]{1,0:T(8,128)(2,1)} %kv.1, s32[1,128]{1,0:T(1,128)} %bitcast.7, s32[64]{0:T(128)} %groups.1, bf16[4,128,2048]{2,1,0:T(8,128)(2,1)} %pool.1, s32[4,8]{1,0:T(4,128)} %table.1, ...), custom_call_target="tpu_custom_call" | custom-call | tf_op jit(solution)/shard_map/layer/pallas_call | solution.py:379
  66.2 1.7 %copy.18 = bf16[128,1024]{1,0:T(8,128)(2,1)} copy(bf16[128,1024]{1,0:T(8,128)(2,1)} %get-tuple-element.4) | data formatting | bytes 524288
  67.9 1.7 %copy.19 = bf16[128,1024]{1,0:T(8,128)(2,1)} copy(bf16[128,1024]{1,0:T(8,128)(2,1)} %get-tuple-element.5) | data formatting | bytes 524288
